TPU v7x, 1024 devices: a whole 8x8x8 slice. The times are simulated.
1024 devices in a mesh: gx: 64 (over z, y), gy: 16 (over x, core).
Axes of the slice: x: 8, y: 8, z: 8, core: 2. Of those that a mesh axis runs over, the one named last changes fastest.
Arguments:
- tokens: bfloat16 [128, 16384], P('gy', 'gx'), may hold values from -6 to 6
- gate_weight: bfloat16 [16384, 32768], P('gx', 'gy'), may hold values from -0.046875 to 0.046875
- up_weight: bfloat16 [16384, 32768], P('gx', 'gy'), may hold values from -0.046875 to 0.046875
- gate_scale: float32 [32768], P('gy'), may hold values from 0.1 to 1.9
- up_scale: float32 [32768], P('gy'), may hold values from 0.1 to 1.9
- down_weight: bfloat16 [32768, 16384], P('gy', 'gx'), may hold values from -0.03125 to 0.03125
- down_scale: float32 [16384], P('gx'), may hold values from 0.1 to 1.9
Outputs:
- result: bfloat16 [128, 16384], P('gy', 'gx')
All inputs are finite; a program needn't handle non-finite values.
Results may differ from a plain program's by a relative error of at most 0.011.
Values may be sent and summed in bfloat16 or wider, within the bound.
A program may use at most 32 MiB of HBM per device.

v0:
```python
import jax
import jax.numpy as jnp
from jax import lax
from jax.sharding import PartitionSpec as P


def local(tokens, gate_weight, up_weight, gate_scale, up_scale, down_weight, down_scale):
    gathered = lax.all_gather(tokens, "gy", axis=0, tiled=True)
    hidden_width = gate_weight.shape[1]
    gate_part = jnp.dot(gathered, gate_weight, preferred_element_type=jnp.float32)
    up_part = jnp.dot(gathered, up_weight, preferred_element_type=jnp.float32)
    summed = lax.psum_scatter(
        jnp.concatenate([gate_part, up_part], axis=1), "gx", scatter_dimension=0, tiled=True
    )
    gate_act = summed[:, :hidden_width] * gate_scale
    up_act = summed[:, hidden_width:] * up_scale
    hidden = (jax.nn.silu(gate_act) * up_act).astype(jnp.bfloat16)
    partials = jnp.dot(
        lax.all_gather(hidden, "gx", axis=0, tiled=True),
        down_weight,
        preferred_element_type=jnp.float32,
    )
    reduced = lax.psum_scatter(partials, "gy", scatter_dimension=0, tiled=True)
    return (reduced * down_scale).astype(jnp.bfloat16)


def solution(mesh):
    return jax.shard_map(
        local,
        mesh=mesh,
        in_specs=(
            P("gy", "gx"),
            P("gx", "gy"),
            P("gx", "gy"),
            P("gy"),
            P("gy"),
            P("gy", "gx"),
            P("gx"),
        ),
        out_specs=P("gy", "gx"),
        check_vma=False,
    )
```

profile of v0, /device:TPU:1, one launch (start us, length us, event | category | flops | bytes accessed | tf_op | source)
XLA Modules:
  0.0 328.8 jit_solution(1304902814998408610)
XLA Ops:
  6.5 0.0 copy-start
  6.5 0.0 copy-start.1
  6.5 0.0 all-reduce.3.cloned.1.call-start
  6.5 28.7 %all_gather.6 = bf16[128,256]{1,0:T(8,128)(2,1)S(1)} all-gather(bf16[8,256]{1,0:T(8,128)(2,1)} %param.7), channel_id=1, replica_groups=mesh['gx'=64,'gy'=16] {'gy'}, dimensions={0}, use_global_device_ids=true | all-gather | bytes 69632 | tf_op jit(solution)/shard_map/all_gather | solution.py:8
  35.3 0.0 copy-done
  35.3 0.3 fusion.3
  35.6 0.0 copy-done.1
  35.6 0.3 fusion.4
  35.9 1.5 pad_maximum_fusion
  37.4 0.0 copy-start.3
  37.4 0.0 copy-start.4
  37.4 0.0 copy-start.2
  37.4 0.0 all-reduce.3.cloned.1.call-update
  37.4 0.0 copy-start.5
  37.4 0.0 reduce-scatter.2.cloned.1.call-start
  37.5 1.4 dynamic-slice
  39.5 170.5 %all-reduce.3.cloned.1.call-done = f32[128,4096]{1,0:T(8,128)} async-done(((f32[128,4096]{1,0:T(8,128)}), f32[128,4096]{1,0:T(8,128)}) %all-reduce.3.cloned.1.call-update) | async-done | bytes 2097168
  209.9 0.0 copy-done.3
  209.9 0.0 copy-done.4
  209.9 1.0 fusion.2
  210.9 35.6 %all-gather = bf16[64,2,2048]{2,1,0:T(2,128)(2,1)S(1)} all-gather(bf16[1,2,2048]{2,1,0:T(2,128)(2,1)S(1)} %fusion.2), channel_id=1, replica_groups=mesh['gx'=64,'gy'=16] {'gx'}, dimensions={0}, use_global_device_ids=true | all-gather | bytes 532480 | tf_op jit(solution)/shard_map/all_gather | solution.py:19
  246.5 0.2 reshape.4
  246.7 0.0 copy-done.2
  246.7 1.0 fusion.5
  247.6 0.0 reduce-scatter.2.cloned.1.call-update
  247.7 73.0 %reduce-scatter.2.cloned.1.call-done = f32[8,256]{1,0:T(8,128)} async-done(((f32[128,256]{1,0:T(8,128)}), f32[8,256]{1,0:T(8,128)}) %reduce-scatter.2.cloned.1.call-update) | async-done | bytes 8208 | tf_op jit(solution)/shard_map/reduce_scatter | solution.py:23
  320.7 0.0 copy-done.5
  320.7 1.3 multiply_convert_fusion
Async XLA Ops:
  6.5 28.7 %copy-start = (bf16[256,2048]{1,0:T(8,128)(2,1)S(1)}, bf16[256,2048]{1,0:T(8,128)(2,1)}, u32[]{:S(2)}) copy-start(bf16[256,2048]{1,0:T(8,128)(2,1)} %param.8) | copy-start | bytes 3145732
  6.5 29.0 %copy-start.1 = (bf16[256,2048]{1,0:T(8,128)(2,1)S(1)}, bf16[256,2048]{1,0:T(8,128)(2,1)}, u32[]{:S(2)}) copy-start(bf16[256,2048]{1,0:T(8,128)(2,1)} %param.9) | copy-start | bytes 3145732
  6.5 203.4 %all-reduce.3.cloned.1.call-start = ((), (), s32[]{:S(2)}) async-start(), calls=%async_computation.2 | async-start | bytes 4194304
  37.4 172.6 %copy-start.3 = (f32[2048]{0:T(1024)S(1)}, f32[2048]{0:T(1024)}, u32[]{:S(2)}) copy-start(f32[2048]{0:T(1024)} %param.11) | copy-start | bytes 24580
  37.4 172.6 %copy-start.4 = (f32[2048]{0:T(1024)S(1)}, f32[2048]{0:T(1024)}, u32[]{:S(2)}) copy-start(f32[2048]{0:T(1024)} %param.10) | copy-start | bytes 24580
  37.4 209.3 %copy-start.2 = (bf16[2048,256]{1,0:T(8,128)(2,1)S(1)}, bf16[2048,256]{1,0:T(8,128)(2,1)}, u32[]{:S(2)}) copy-start(bf16[2048,256]{1,0:T(8,128)(2,1)} %param.12) | copy-start | bytes 3145732
  37.4 283.3 %copy-start.5 = (f32[256]{0:T(256)S(1)}, f32[256]{0:T(256)}, u32[]{:S(2)}) copy-start(f32[256]{0:T(256)} %param.13) | copy-start | bytes 3076
  37.4 283.2 %reduce-scatter.2.cloned.1.call-start = ((), (), s32[]{:S(2)}) async-start(), calls=%async_computation.1 | async-start | bytes 139264 | tf_op jit(solution)/shard_map/reduce_scatter | solution.py:23
Sparse Core Ops, SparseCore 0:
  37.5 172.3 all-reduce.2
  247.8 72.8 reduce-scatter.1
where the time goes:
time: 329 us
  waiting for transfers between devices  243 us (74%)
  blocking collectives  64.3 us (20%)
  between operations  14.1 us (4%)
  other arithmetic  3.72 us (1%)
    unnamed x3, waiting for transfers between devices  170 us
    reduce_scatter x1, waiting for transfers between devices, local(): reduced = lax.psum_scatter(partials, 'gy', scatter_dimension=0, tiled=True)  73 us
    all_gather x1, blocking collectives, local(): lax.all_gather(hidden, 'gx', axis=0, tiled=True)  35.6 us
    all_gather x1, blocking collectives, local(): gathered = lax.all_gather(tokens, 'gy', axis=0, tiled=True)  28.7 us
  transfers between devices with their start and end apart: 2, of which 2 were waited for; matrix products, arithmetic and copies ran while one was open for 0% of the time, Pallas kernels for 0%

commit v1 on v0

v1 whole, which is shorter than its diff:
```python
import functools

import jax
import jax.numpy as jnp
from jax import lax
from jax.experimental import pallas as pl
from jax.experimental.pallas import tpu as pltpu
from jax.sharding import PartitionSpec as P

MESH = pl.DeviceIdType.MESH
F32, BF16 = jnp.float32, jnp.bfloat16


def far_first(n):
    return sorted(range(1, n), key=lambda d: -min(d, n - d))


def near_first(n):
    return far_first(n)[::-1]


def kernel(n, m, tokens_hbm, gate_hbm, up_hbm, gate_scale_hbm, up_scale_hbm, down_hbm, down_scale_hbm, out_ref,
           tokens_own, gate_w, up_w, gate_s, up_s, down_w, down_s,
           packed, gathered, part, got1, total, sums1, got2, hidden, last, got3,
           load_sem, tok_send, tok_recv, r1_send, r1_recv, r2_send, r2_recv, g1_send, g1_recv, g2_send, g2_recv, f_send, f_recv):
    gx, gy = lax.axis_index("gx"), lax.axis_index("gy")
    z, y = gx // n, lax.rem(gx, n)
    half = 128 * n

    def along(axis, d):
        if axis == 0:
            return (z * n + lax.rem(y + d, n), gy)
        return (lax.rem(z + d, n) * n + y, gy)

    def along_gy(d):
        return (gx, lax.rem(gy + d, m))

    def where(axis, d):
        return lax.rem((y if axis == 0 else z) + d, n)

    def copy(src, dst, send, recv, to):
        return pltpu.make_async_remote_copy(
            src_ref=src, dst_ref=dst, send_sem=send, recv_sem=recv, device_id=to, device_id_type=MESH
        )

    loads = [
        pltpu.make_async_copy(a, b, load_sem.at[i])
        for i, (a, b) in enumerate(
            (
                (tokens_hbm, tokens_own),
                (gate_hbm, gate_w),
                (up_hbm, up_w),
                (gate_scale_hbm, gate_s),
                (up_scale_hbm, up_s),
                (down_hbm, down_w),
                (down_scale_hbm, down_s),
            )
        )
    ]
    for load in loads:
        load.start()

    barrier = pltpu.get_barrier_semaphore()
    for d in range(1, m):
        pl.semaphore_signal(barrier, inc=1, device_id=along_gy(d), device_id_type=MESH)
    for axis in (0, 1):
        for d in range(1, n):
            pl.semaphore_signal(barrier, inc=1, device_id=along(axis, d), device_id_type=MESH)

    loads[0].wait()
    own = tokens_own[...].astype(F32)
    packed[...] = jnp.concatenate([own[:, :128], own[:, 128:]], axis=0).astype(BF16)
    gathered[gy] = packed[...]
    pl.semaphore_wait(barrier, m - 1 + 2 * (n - 1))

    sends = []

    def start(c):
        c.start()
        sends.append(c)

    order = sorted(range(1, m), key=lambda d: -min(d // 2, n - d // 2))
    for d in order:
        start(copy(packed, gathered.at[gy], tok_send.at[d - 1], tok_recv.at[d - 1], along_gy(d)))
    for d in order[::-1]:
        copy(packed, gathered.at[lax.rem(gy + m - d, m)], tok_send.at[d - 1], tok_recv.at[d - 1], along_gy(d)).wait_recv()
    wide = gathered[...].astype(F32)
    x = jnp.concatenate([wide[:, :8].reshape(8 * m, 128), wide[:, 8:].reshape(8 * m, 128)], axis=1).astype(BF16)

    loads[1].wait()
    loads[2].wait()
    for h in (0, 1):
        cols = slice(h * half, (h + 1) * half)
        part[h, :, :, :half] = jnp.dot(x, gate_w[:, cols], preferred_element_type=F32).astype(BF16).reshape(n, 16, half)
        part[h, :, :, half:] = jnp.dot(x, up_w[:, cols], preferred_element_type=F32).astype(BF16).reshape(n, 16, half)
        for d in far_first(n):
            start(copy(part.at[h, where(h, d)], got1.at[h, d - 1], r1_send.at[h, d - 1], r1_recv.at[h, d - 1], along(h, d)))
    for h in (0, 1):
        total[h] = part[h, where(h, 0)].astype(F32)
    order = near_first(n)
    for d in order[:-1]:
        for h in (0, 1):
            copy(part.at[h, 0], got1.at[h, d - 1], r1_send.at[h, d - 1], r1_recv.at[h, d - 1], along(h, d)).wait_recv()
            total[h] += got1[h, d - 1].astype(F32)
    d = order[-1]
    for h in (0, 1):
        copy(part.at[h, 0], got1.at[h, d - 1], r1_send.at[h, d - 1], r1_recv.at[h, d - 1], along(h, d)).wait_recv()
        done = total[h] + got1[h, d - 1].astype(F32)
        for j in range(n):
            sums1[h, j, :, :128] = done[:, j * 128 : j * 128 + 128].astype(BF16)
            sums1[h, j, :, 128:] = done[:, half + j * 128 : half + j * 128 + 128].astype(BF16)
        for e in far_first(n):
            start(copy(sums1.at[h, where(1 - h, e)], got2.at[h, e - 1], r2_send.at[h, e - 1], r2_recv.at[h, e - 1], along(1 - h, e)))

    loads[3].wait()
    loads[4].wait()
    for h in (0, 1):
        i, j = where(h, 0), where(1 - h, 0)
        acc = sums1[h, j].astype(F32)
        for e in near_first(n):
            copy(sums1.at[h, 0], got2.at[h, e - 1], r2_send.at[h, e - 1], r2_recv.at[h, e - 1], along(1 - h, e)).wait_recv()
            acc += got2[h, e - 1].astype(F32)
        gate = acc[:, :128] * gate_s[pl.ds(h * n + j, 1), :]
        up = acc[:, 128:] * up_s[pl.ds(h * n + j, 1), :]
        mine = pl.ds(pl.multiple_of(j * 128, 128), 128)
        hidden[h, i, :, mine] = (gate / (1.0 + jnp.exp(-gate)) * up).astype(BF16)
        for e in far_first(n):
            spot = hidden.at[h, i, :, mine]
            start(copy(spot, spot, g1_send.at[h, e - 1], g1_recv.at[h, e - 1], along(1 - h, e)))
    for h in (0, 1):
        i, j = where(h, 0), where(1 - h, 0)
        for e in near_first(n):
            spot = hidden.at[h, i, :, pl.ds(pl.multiple_of(where(1 - h, n - e) * 128, 128), 128)]
            copy(spot, spot, g1_send.at[h, e - 1], g1_recv.at[h, e - 1], along(1 - h, e)).wait_recv()
        for d in far_first(n):
            spot = hidden.at[h, i]
            start(copy(spot, spot, g2_send.at[h, d - 1], g2_recv.at[h, d - 1], along(h, d)))
    loads[5].wait()
    for h in (0, 1):
        for d in near_first(n):
            spot = hidden.at[h, where(h, n - d)]
            copy(spot, spot, g2_send.at[h, d - 1], g2_recv.at[h, d - 1], along(h, d)).wait_recv()
    result = jnp.dot(hidden[0].reshape(8 * m, half), down_w[:half, :], preferred_element_type=F32)
    result += jnp.dot(hidden[1].reshape(8 * m, half), down_w[half:, :], preferred_element_type=F32)

    pieces = result.reshape(m, 8, 256)
    last[...] = jnp.concatenate([pieces[:, :, :128], pieces[:, :, 128:]], axis=1).astype(BF16)
    order = sorted(range(1, m), key=lambda d: -min(d // 2, n - d // 2))
    for d in order:
        start(copy(last.at[lax.rem(gy + d, m)], got3.at[d - 1], f_send.at[d - 1], f_recv.at[d - 1], along_gy(d)))
    loads[6].wait()
    acc = last[gy].astype(F32)
    for d in order[::-1]:
        copy(last.at[0], got3.at[d - 1], f_send.at[d - 1], f_recv.at[d - 1], along_gy(d)).wait_recv()
        acc += got3[d - 1].astype(F32)
    out_ref[...] = (jnp.concatenate([acc[:8], acc[8:]], axis=1) * down_s[...]).astype(BF16)
    for c in sends:
        c.wait_send()


def solution(mesh):
    n = int(round(mesh.shape["gx"] ** 0.5))
    m = mesh.shape["gy"]
    half = 128 * n
    dma = pltpu.SemaphoreType.DMA

    def local(tokens, gate_weight, up_weight, gate_scale, up_scale, down_weight, down_scale):
        return pl.pallas_call(
            functools.partial(kernel, n, m),
            out_shape=jax.ShapeDtypeStruct((8, 256), BF16),
            in_specs=[pl.BlockSpec(memory_space=pltpu.HBM)] * 7,
            out_specs=pl.BlockSpec(memory_space=pltpu.VMEM),
            scratch_shapes=[
                pltpu.VMEM((8, 256), BF16),
                pltpu.VMEM((256, 2 * half), BF16),
                pltpu.VMEM((256, 2 * half), BF16),
                pltpu.VMEM((2 * n, 128), F32),
                pltpu.VMEM((2 * n, 128), F32),
                pltpu.VMEM((2 * half, 256), BF16),
                pltpu.VMEM((1, 256), F32),
                pltpu.VMEM((16, 128), BF16),
                pltpu.VMEM((m, 16, 128), BF16),
                pltpu.VMEM((2, n, 16, 2 * half), BF16),
                pltpu.VMEM((2, n - 1, 16, 2 * half), BF16),
                pltpu.VMEM((2, 16, 2 * half), F32),
                pltpu.VMEM((2, n, 16, 256), BF16),
                pltpu.VMEM((2, n - 1, 16, 256), BF16),
                pltpu.VMEM((2, n, 16, half), BF16),
                pltpu.VMEM((m, 16, 128), BF16),
                pltpu.VMEM((m - 1, 16, 128), BF16),
                dma((7,)),
                dma((m - 1,)),
                dma((m - 1,)),
                *([dma((2, n - 1))] * 8),
                dma((m - 1,)),
                dma((m - 1,)),
            ],
            compiler_params=pltpu.CompilerParams(
                collective_id=0, has_side_effects=True, vmem_limit_bytes=60 << 20
            ),
            name="feed_forward",
        )(
            tokens,
            gate_weight,
            up_weight,
            gate_scale.reshape(2 * n, 128),
            up_scale.reshape(2 * n, 128),
            down_weight,
            down_scale.reshape(1, 256),
        )

    return jax.shard_map(
        local,
        mesh=mesh,
        in_specs=(P("gy", "gx"), P("gx", "gy"), P("gx", "gy"), P("gy"), P("gy"), P("gy", "gx"), P("gx")),
        out_specs=P("gy", "gx"),
        check_vma=False,
    )
```

time: 329 us -> 67 us (0.20)
  waiting for transfers between devices: 243 us -> 0 us
  Pallas kernels: 0 us -> 65.5 us
  blocking collectives: 64.3 us -> 0 us
  between operations: 14.1 us -> 0.01 us
  other arithmetic: 3.72 us -> 0 us
    unnamed x3 -> x0, waiting for transfers between devices: 170 us -> none
    reduce_scatter x1 -> x0, waiting for transfers between devices: 73 us -> none  [local(): reduced = lax.psum_scatter(partials, 'gy', scatter_dimension=0, tiled=True)]
    pallas_call x0 -> x1, Pallas kernels: none -> 65.5 us  [local(): pl.pallas_call(functools.partial(kernel, n, m), out_shape=jax.ShapeDtypeS...]
    all_gather x2 -> x0, blocking collectives: 64.3 us -> none  [the longest x1 35.6 us: local(): lax.all_gather(hidden, 'gx', axis=0, tiled=True)]
  transfers between devices with their start and end apart: 2 -> 0, of which waited for: 2 -> 0; matrix products, arithmetic and copies ran while one was open for 0% -> 0% of each run, Pallas kernels for 0% -> 0%
where the time goes in v1:
time: 67 us; the launch traced here: 66.8 us
  Pallas kernels  65.5 us (98%)
  local copies, waits for them, and re-layouts  1.28 us (2%)
    pallas_call x1, Pallas kernels, local(): pl.pallas_call(functools.partial(kernel, n, m), out_shape=jax.ShapeDtypeS...  65.5 us

profile of v1, /device:TPU:1, one launch (start us, length us, event | category | flops | bytes accessed | tf_op | source)
XLA Modules:
  0.0 66.8 jit_solution(15952124908760228576)
XLA Ops:
  0.0 65.5 %feed_forward.1 = bf16[8,256]{1,0:T(8,128)(2,1)} custom-call(bf16[8,256]{1,0:T(8,128)(2,1)} %tokens_hbm.1, bf16[256,2048]{1,0:T(8,128)(2,1)} %gate_hbm.1, bf16[256,2048]{1,0:T(8,128)(2,1)} %up_hbm.1, f32[16,128]{1,0:T(8,128)} %bitcast.3, f32[16,128]{1,0:T(8,128)} %bitcast.4, bf16[2048,256]{1,0:T(8,128)(2,1)} %down_hbm.1, f32[1,256]{1,0:T(1,128)} %bitcast.5), custom_call_target="tpu_custom_call" | custom-call | tf_op jit(solution)/shard_map/feed_forward/pallas_call | solution.py:168
  65.5 1.3 %copy.9 = bf16[8,256]{1,0:T(8,128)(2,1)} copy(bf16[8,256]{1,0:T(8,128)(2,1)} %feed_forward.1) | data formatting | bytes 8192

commit v2 on v0

v2 whole, which is shorter than its diff:
```python
import functools

import jax
import jax.numpy as jnp
from jax import lax
from jax.experimental import pallas as pl
from jax.experimental.pallas import tpu as pltpu
from jax.sharding import PartitionSpec as P

MESH = pl.DeviceIdType.MESH
F32, BF16 = jnp.float32, jnp.bfloat16


def far_first(n):
    return sorted(range(1, n), key=lambda d: -min(d, n - d))


def cut(n, parts):
    return [(n * k // parts, n * (k + 1) // parts) for k in range(parts)]


CHUNKS = 3
GROUPS = 3


def kernel(n, m, chunks, groups, tokens_hbm, gate_hbm, up_hbm, gate_scale_hbm, up_scale_hbm, down_hbm, down_scale_hbm, out_ref,
           tokens_own, weights, gate_s, up_s, down_w, down_s, packed, gathered, *rest):
    parts, rest = rest[: len(chunks)], rest[len(chunks) :]
    got1, rest = rest[: len(chunks)], rest[len(chunks) :]
    sums1, got2 = rest[:2]
    hidden, rest = rest[2 : 2 + len(groups)], rest[2 + len(groups) :]
    last, got3, load_sem, tok_sem, r1_sem, r2_sem, g1_sem, g2_sem, f_sem = rest
    gx, gy = lax.axis_index("gx"), lax.axis_index("gy")
    z, y = gx // n, lax.rem(gx, n)
    to_send = far_first(n) + [0]
    to_keep = to_send[::-1]

    def place(q):
        for g, (a, b) in enumerate(groups):
            if a <= q < b:
                return g, q - a

    def along(axis, d):
        if axis == 0:
            return (z * n + lax.rem(y + d, n), gy)
        return (lax.rem(z + d, n) * n + y, gy)

    def along_gy(d):
        return (gx, lax.rem(gy + d, m))

    def where(axis, d):
        return lax.rem((y if axis == 0 else z) + d, n)

    def send(src, dst, sems, to):
        pltpu.make_async_remote_copy(
            src_ref=src, dst_ref=dst, send_sem=sems.at[0], recv_sem=sems.at[1], device_id=to, device_id_type=MESH
        ).start()

    def wait(sem, like):
        pltpu.make_async_copy(like, like, sem).wait()

    barrier = pltpu.get_barrier_semaphore()
    load_tokens = pltpu.make_async_copy(tokens_hbm, tokens_own, load_sem.at[0])
    load_tokens.start()
    by_distance = sorted(range(1, m), key=lambda d: -min(d // 2, n - d // 2))
    for d in by_distance:
        pl.semaphore_signal(barrier, inc=1, device_id=along_gy(d), device_id_type=MESH)
    for d in far_first(n):
        for axis in (0, 1):
            pl.semaphore_signal(barrier, inc=1, device_id=along(axis, d), device_id_type=MESH)

    for h in (0, 1):
        for p, e in enumerate(to_send):
            block = pl.ds(pl.multiple_of((h * n + where(1 - h, e)) * 128, 128), 128)
            pltpu.make_async_copy(gate_hbm.at[:, block], weights.at[h, :, pl.ds(p * 256, 128)], load_sem.at[1]).start()
            pltpu.make_async_copy(up_hbm.at[:, block], weights.at[h, :, pl.ds(p * 256 + 128, 128)], load_sem.at[1]).start()

    load_tokens.wait()
    own = tokens_own[...].astype(F32)
    packed[...] = jnp.concatenate([own[:, :128], own[:, 128:]], axis=0).astype(BF16)
    gathered[gy] = packed[...]
    pl.semaphore_wait(barrier, m - 1 + 2 * (n - 1))
    for d in by_distance:
        send(packed, gathered.at[gy], tok_sem, along_gy(d))
    for h in (0, 1):
        for q, e in enumerate(to_keep):
            block = pl.ds(pl.multiple_of((h * n + where(1 - h, e)) * 128, 128), 128)
            pltpu.make_async_copy(down_hbm.at[block, :], down_w.at[pl.ds((h * n + q) * 128, 128), :], load_sem.at[2]).start()
    small = [
        pltpu.make_async_copy(a, b, load_sem.at[3 + k])
        for k, (a, b) in enumerate(((gate_scale_hbm, gate_s), (up_scale_hbm, up_s), (down_scale_hbm, down_s)))
    ]
    for load in small:
        load.start()
    wait(load_sem.at[1], weights)
    wait(tok_sem.at[1], gathered.at[pl.ds(0, m - 1)])
    wide = gathered[...].astype(F32)
    x = jnp.concatenate([wide[:, :8].reshape(8 * m, 128), wide[:, 8:].reshape(8 * m, 128)], axis=1).astype(BF16)

    for c, (a, b) in enumerate(chunks):
        for h in (0, 1):
            sums = jnp.dot(x, weights[h, :, a * 256 : b * 256], preferred_element_type=F32)
            parts[c][h] = sums.astype(BF16).reshape(n, 16, (b - a) * 256)
            for d in far_first(n):
                send(parts[c].at[h, where(h, d)], got1[c].at[h, d - 1], r1_sem.at[h, c], along(h, d))
    wait(tok_sem.at[0], gathered.at[pl.ds(0, m - 1)])
    for load in small:
        load.wait()
    wait(load_sem.at[2], down_w)
    for c, (a, b) in enumerate(chunks):
        for h in (0, 1):
            wait(r1_sem.at[h, c, 1], got1[c].at[h])
            acc = parts[c][h, where(h, 0)].astype(F32)
            for d in range(1, n):
                acc += got1[c][h, d - 1].astype(F32)
            for p in range(a, b):
                sums1[h, p] = acc[:, (p - a) * 256 : (p - a + 1) * 256].astype(BF16)
            for p in range(a, b):
                if to_send[p]:
                    send(sums1.at[h, p], got2.at[h, p], r2_sem.at[h], along(1 - h, to_send[p]))

    for c in range(len(chunks)):
        for h in (0, 1):
            wait(r1_sem.at[h, c, 0], got1[c].at[h])
    for h in (0, 1):
        i, j = where(h, 0), where(1 - h, 0)
        wait(r2_sem.at[h, 1], got2.at[h])
        acc = sums1[h, n - 1].astype(F32)
        for p in range(n - 1):
            acc += got2[h, p].astype(F32)
        gate = acc[:, :128] * gate_s[pl.ds(h * n + j, 1), :]
        up = acc[:, 128:] * up_s[pl.ds(h * n + j, 1), :]
        hidden[0][h, i, 0] = (gate / (1.0 + jnp.exp(-gate)) * up).astype(BF16)
        for f in far_first(n):
            g, k = place(to_keep.index(n - f))
            send(hidden[0].at[h, i, 0], hidden[g].at[h, i, k], g1_sem.at[h, to_keep.index(n - f)], along(1 - h, f))
    for h in (0, 1):
        wait(r2_sem.at[h, 0], got2.at[h])
    for g, (a, b) in enumerate(groups):
        for h in (0, 1):
            i = where(h, 0)
            for q in range(max(a, 1), b):
                wait(g1_sem.at[h, q, 1], hidden[g].at[h, i, q - a])
            for d in far_first(n):
                send(hidden[g].at[h, i], hidden[g].at[h, i], g2_sem.at[h, g], along(h, d))
    for h in (0, 1):
        for q in range(1, n):
            wait(g1_sem.at[h, q, 0], hidden[0].at[h, 0, 0])
    result = jnp.zeros((8 * m, 256), F32)
    for g, (a, b) in enumerate(groups):
        for h in (0, 1):
            wait(g2_sem.at[h, g, 1], hidden[g].at[h, pl.ds(0, n - 1)])
            left = jnp.concatenate([hidden[g][h, :, k].reshape(8 * m, 128) for k in range(b - a)], axis=1)
            result += jnp.dot(left, down_w[(h * n + a) * 128 : (h * n + b) * 128, :], preferred_element_type=F32)

    pieces = result.reshape(m, 8, 256)
    last[...] = jnp.concatenate([pieces[:, :, :128], pieces[:, :, 128:]], axis=1).astype(BF16)
    for d in by_distance:
        send(last.at[lax.rem(gy + d, m)], got3.at[d - 1], f_sem, along_gy(d))
    for g in range(len(groups)):
        for h in (0, 1):
            wait(g2_sem.at[h, g, 0], hidden[g].at[h, pl.ds(0, n - 1)])
    acc = last[gy].astype(F32)
    wait(f_sem.at[1], got3)
    acc += jnp.sum(got3[...].astype(F32), axis=0)
    out_ref[...] = (jnp.concatenate([acc[:8], acc[8:]], axis=1) * down_s[...]).astype(BF16)
    wait(f_sem.at[0], got3)


def solution(mesh):
    n = int(round(mesh.shape["gx"] ** 0.5))
    m = mesh.shape["gy"]
    chunks, groups = cut(n, CHUNKS), cut(n, GROUPS)
    half = 128 * n
    dma = pltpu.SemaphoreType.DMA

    def local(tokens, gate_weight, up_weight, gate_scale, up_scale, down_weight, down_scale):
        return pl.pallas_call(
            functools.partial(kernel, n, m, chunks, groups),
            out_shape=jax.ShapeDtypeStruct((8, 256), BF16),
            in_specs=[pl.BlockSpec(memory_space=pltpu.HBM)] * 7,
            out_specs=pl.BlockSpec(memory_space=pltpu.VMEM),
            scratch_shapes=[
                pltpu.VMEM((8, 256), BF16),
                pltpu.VMEM((2, 256, 2 * half), BF16),
                pltpu.VMEM((2 * n, 128), F32),
                pltpu.VMEM((2 * n, 128), F32),
                pltpu.VMEM((2 * half, 256), BF16),
                pltpu.VMEM((1, 256), F32),
                pltpu.VMEM((16, 128), BF16),
                pltpu.VMEM((m, 16, 128), BF16),
                *[pltpu.VMEM((2, n, 16, (b - a) * 256), BF16) for a, b in chunks],
                *[pltpu.VMEM((2, n - 1, 16, (b - a) * 256), BF16) for a, b in chunks],
                pltpu.VMEM((2, n, 16, 256), BF16),
                pltpu.VMEM((2, n - 1, 16, 256), BF16),
                *[pltpu.VMEM((2, n, b - a, 16, 128), BF16) for a, b in groups],
                pltpu.VMEM((m, 16, 128), BF16),
                pltpu.VMEM((m - 1, 16, 128), BF16),
                dma((6,)),
                dma((2,)),
                dma((2, len(chunks), 2)),
                dma((2, 2)),
                dma((2, n, 2)),
                dma((2, len(groups), 2)),
                dma((2,)),
            ],
            compiler_params=pltpu.CompilerParams(
                collective_id=0, has_side_effects=True, vmem_limit_bytes=60 << 20
            ),
            name="feed_forward",
        )(
            tokens,
            gate_weight,
            up_weight,
            gate_scale.reshape(2 * n, 128),
            up_scale.reshape(2 * n, 128),
            down_weight,
            down_scale.reshape(1, 256),
        )

    return jax.shard_map(
        local,
        mesh=mesh,
        in_specs=(P("gy", "gx"), P("gx", "gy"), P("gx", "gy"), P("gy"), P("gy"), P("gy", "gx"), P("gx")),
        out_specs=P("gy", "gx"),
        check_vma=False,
    )
```

time: 329 us -> 64.5 us (0.20)
  waiting for transfers between devices: 243 us -> 0 us
  blocking collectives: 64.3 us -> 0 us
  Pallas kernels: 0 us -> 63 us
  between operations: 14.1 us -> 0.01 us
  other arithmetic: 3.72 us -> 0 us
    unnamed x3 -> x0, waiting for transfers between devices: 170 us -> none
    reduce_scatter x1 -> x0, waiting for transfers between devices: 73 us -> none  [local(): reduced = lax.psum_scatter(partials, 'gy', scatter_dimension=0, tiled=True)]
    all_gather x2 -> x0, blocking collectives: 64.3 us -> none  [the longest x1 35.6 us: local(): lax.all_gather(hidden, 'gx', axis=0, tiled=True)]
    pallas_call x0 -> x1, Pallas kernels: none -> 63 us  [local(): pl.pallas_call(functools.partial(kernel, n, m, chunks, groups), out_shape...]
  transfers between devices with their start and end apart: 2 -> 0, of which waited for: 2 -> 0; matrix products, arithmetic and copies ran while one was open for 0% -> 0% of each run, Pallas kernels for 0% -> 0%
where the time goes in v2:
time: 64.5 us; the launch traced here: 64.3 us
  Pallas kernels  63 us (98%)
  local copies, waits for them, and re-layouts  1.28 us (2%)
    pallas_call x1, Pallas kernels, local(): pl.pallas_call(functools.partial(kernel, n, m, chunks, groups), out_shape...  63 us

profile of v2, /device:TPU:1, one launch (start us, length us, event | category | flops | bytes accessed | tf_op | source)
XLA Modules:
  0.0 64.3 jit_solution(10872658386063925179)
XLA Ops:
  0.0 63.0 %feed_forward.1 = bf16[8,256]{1,0:T(8,128)(2,1)} custom-call(bf16[8,256]{1,0:T(8,128)(2,1)} %tokens_hbm.1, bf16[256,2048]{1,0:T(8,128)(2,1)} %gate_hbm.1, bf16[256,2048]{1,0:T(8,128)(2,1)} %up_hbm.1, f32[16,128]{1,0:T(8,128)} %bitcast.3, f32[16,128]{1,0:T(8,128)} %bitcast.4, bf16[2048,256]{1,0:T(8,128)(2,1)} %down_hbm.1, f32[1,256]{1,0:T(1,128)} %bitcast.5), custom_call_target="tpu_custom_call" | custom-call | tf_op jit(solution)/shard_map/feed_forward/pallas_call | solution.py:178
  63.0 1.3 %copy.9 = bf16[8,256]{1,0:T(8,128)(2,1)} copy(bf16[8,256]{1,0:T(8,128)(2,1)} %feed_forward.1) | data formatting | bytes 8192

commit v3 on v2

--- a/solution.py
+++ b/solution.py
@@ -15,6 +15,12 @@
     return sorted(range(1, n), key=lambda d: -min(d, n - d))
 
 
+def routes(n):
+    if n == 8:
+        return [(-4, -2), (-3, -1)], [(3, 1)], [-1, 1]
+    return [], [], list(range(1, n))
+
+
 def cut(n, parts):
     return [(n * k // parts, n * (k + 1) // parts) for k in range(parts)]
 
@@ -27,9 +33,11 @@
            tokens_own, weights, gate_s, up_s, down_w, down_s, packed, gathered, *rest):
     parts, rest = rest[: len(chunks)], rest[len(chunks) :]
     got1, rest = rest[: len(chunks)], rest[len(chunks) :]
+    relayed, rest = rest[: len(chunks)], rest[len(chunks) :]
+    passed, rest = rest[: len(chunks)], rest[len(chunks) :]
     sums1, got2 = rest[:2]
     hidden, rest = rest[2 : 2 + len(groups)], rest[2 + len(groups) :]
-    last, got3, load_sem, tok_sem, r1_sem, r2_sem, g1_sem, g2_sem, f_sem = rest
+    last, got3, load_sem, tok_sem, rl_sem, r1_sem, r2_sem, g1_sem, g2_sem, f_sem = rest
     gx, gy = lax.axis_index("gx"), lax.axis_index("gy")
     z, y = gx // n, lax.rem(gx, n)
     to_send = far_first(n) + [0]
@@ -47,6 +55,11 @@
 
     def along_gy(d):
         return (gx, lax.rem(gy + d, m))
+
+    side = 1 - 2 * lax.rem(gy, 2)
+
+    def turned(d):
+        return lax.rem(side * d + 2 * n, n)
 
     def where(axis, d):
         return lax.rem((y if axis == 0 else z) + d, n)
@@ -97,22 +110,35 @@
     wide = gathered[...].astype(F32)
     x = jnp.concatenate([wide[:, :8].reshape(8 * m, 128), wide[:, 8:].reshape(8 * m, 128)], axis=1).astype(BF16)
 
+    ahead, behind, direct = routes(n)
     for c, (a, b) in enumerate(chunks):
         for h in (0, 1):
             sums = jnp.dot(x, weights[h, :, a * 256 : b * 256], preferred_element_type=F32)
             parts[c][h] = sums.astype(BF16).reshape(n, 16, (b - a) * 256)
-            for d in far_first(n):
-                send(parts[c].at[h, where(h, d)], got1[c].at[h, d - 1], r1_sem.at[h, c], along(h, d))
+            for s, (far, stop) in enumerate(ahead + behind):
+                send(parts[c].at[h, where(h, turned(far))], relayed[c].at[h, s], rl_sem.at[h, c], along(h, turned(stop)))
+            for s, d in enumerate(direct):
+                send(parts[c].at[h, where(h, turned(d))], got1[c].at[h, s], r1_sem.at[h, c], along(h, turned(d)))
     wait(tok_sem.at[0], gathered.at[pl.ds(0, m - 1)])
     for load in small:
         load.wait()
     wait(load_sem.at[2], down_w)
+    for c in range(len(chunks)):
+        for h in (0, 1):
+            if ahead:
+                wait(rl_sem.at[h, c, 1], relayed[c].at[h])
+                for s, (d, first, count) in enumerate(((-2, 0, len(ahead)), (2, len(ahead), len(behind)))):
+                    acc = parts[c][h, where(h, turned(d))].astype(F32)
+                    for k in range(first, first + count):
+                        acc += relayed[c][h, k].astype(F32)
+                    passed[c][h, s] = acc.astype(BF16)
+                    send(passed[c].at[h, s], got1[c].at[h, len(direct) + s], r1_sem.at[h, c], along(h, turned(d)))
     for c, (a, b) in enumerate(chunks):
         for h in (0, 1):
             wait(r1_sem.at[h, c, 1], got1[c].at[h])
             acc = parts[c][h, where(h, 0)].astype(F32)
-            for d in range(1, n):
-                acc += got1[c][h, d - 1].astype(F32)
+            for k in range(got1[c].shape[1]):
+                acc += got1[c][h, k].astype(F32)
             for p in range(a, b):
                 sums1[h, p] = acc[:, (p - a) * 256 : (p - a + 1) * 256].astype(BF16)
             for p in range(a, b):
@@ -122,6 +148,8 @@
     for c in range(len(chunks)):
         for h in (0, 1):
             wait(r1_sem.at[h, c, 0], got1[c].at[h])
+            if ahead:
+                wait(rl_sem.at[h, c, 0], relayed[c].at[h])
     for h in (0, 1):
         i, j = where(h, 0), where(1 - h, 0)
         wait(r2_sem.at[h, 1], got2.at[h])
@@ -171,13 +199,16 @@
     n = int(round(mesh.shape["gx"] ** 0.5))
     m = mesh.shape["gy"]
     chunks, groups = cut(n, CHUNKS), cut(n, GROUPS)
+    ahead, behind, direct = routes(n)
+    relays = len(ahead) + len(behind)
+    arrivals = len(direct) + (2 if relays else 0)
     half = 128 * n
     dma = pltpu.SemaphoreType.DMA
 
     def local(tokens, gate_weight, up_weight, gate_scale, up_scale, down_weight, down_scale):
         return pl.pallas_call(
             functools.partial(kernel, n, m, chunks, groups),
-            out_shape=jax.ShapeDtypeStruct((8, 256), BF16),
+            out_shape=pltpu.VMEM((8, 256), BF16),
             in_specs=[pl.BlockSpec(memory_space=pltpu.HBM)] * 7,
             out_specs=pl.BlockSpec(memory_space=pltpu.VMEM),
             scratch_shapes=[
@@ -190,7 +221,9 @@
                 pltpu.VMEM((16, 128), BF16),
                 pltpu.VMEM((m, 16, 128), BF16),
                 *[pltpu.VMEM((2, n, 16, (b - a) * 256), BF16) for a, b in chunks],
-                *[pltpu.VMEM((2, n - 1, 16, (b - a) * 256), BF16) for a, b in chunks],
+                *[pltpu.VMEM((2, arrivals, 16, (b - a) * 256), BF16) for a, b in chunks],
+                *[pltpu.VMEM((2, max(1, relays), 16, (b - a) * 256), BF16) for a, b in chunks],
+                *[pltpu.VMEM((2, 2, 16, (b - a) * 256), BF16) for a, b in chunks],
                 pltpu.VMEM((2, n, 16, 256), BF16),
                 pltpu.VMEM((2, n - 1, 16, 256), BF16),
                 *[pltpu.VMEM((2, n, b - a, 16, 128), BF16) for a, b in groups],
@@ -198,6 +231,7 @@
                 pltpu.VMEM((m - 1, 16, 128), BF16),
                 dma((6,)),
                 dma((2,)),
+                dma((2, len(chunks), 2)),
                 dma((2, len(chunks), 2)),
                 dma((2, 2)),
                 dma((2, n, 2)),

time: 64.5 us -> 59.9 us (0.929)
  Pallas kernels: 63 us -> 59.1 us
  local copies, waits for them, and re-layouts: 1.28 us -> 0.6 us
    pallas_call x1, Pallas kernels: 63 us -> 59.1 us  [local(): pl.pallas_call(functools.partial(kernel, n, m, chunks, groups), out_shape...]
    unnamed x1, local copies, waits for them, and re-layouts: 1.28 us -> 0.6 us
where the time goes in v3:
time: 59.9 us; the launch traced here: 59.7 us
  Pallas kernels  59.1 us (99%)
  local copies, waits for them, and re-layouts  0.6 us (1%)
    pallas_call x1, Pallas kernels, local(): pl.pallas_call(functools.partial(kernel, n, m, chunks, groups), out_shape...  59.1 us

profile of v3, /device:TPU:1, one launch (start us, length us, event | category | flops | bytes accessed | tf_op | source)
XLA Modules:
  0.0 59.7 jit_solution(3320464395331398391)
XLA Ops:
  0.0 59.1 %feed_forward.1 = bf16[8,256]{1,0:T(8,128)(2,1)S(1)} custom-call(bf16[8,256]{1,0:T(8,128)(2,1)} %tokens_hbm.1, bf16[256,2048]{1,0:T(8,128)(2,1)} %gate_hbm.1, bf16[256,2048]{1,0:T(8,128)(2,1)} %up_hbm.1, f32[16,128]{1,0:T(8,128)} %bitcast.3, f32[16,128]{1,0:T(8,128)} %bitcast.4, bf16[2048,256]{1,0:T(8,128)(2,1)} %down_hbm.1, f32[1,256]{1,0:T(1,128)} %bitcast.5), custom_call_target="tpu_custom_call" | custom-call | tf_op jit(solution)/shard_map/feed_forward/pallas_call | solution.py:209
  59.1 0.6 copy.9

commit v4 on v3

--- a/solution.py
+++ b/solution.py
@@ -21,12 +21,15 @@
     return [], [], list(range(1, n))
 
 
+def by_hops(n):
+    return [(0, 1)] + [(2 * k - 1, min(2 * k + 1, n)) for k in range(1, n // 2 + 1)]
+
+
 def cut(n, parts):
     return [(n * k // parts, n * (k + 1) // parts) for k in range(parts)]
 
 
-CHUNKS = 3
-GROUPS = 3
+CHUNKS = 4
 
 
 def kernel(n, m, chunks, groups, tokens_hbm, gate_hbm, up_hbm, gate_scale_hbm, up_scale_hbm, down_hbm, down_scale_hbm, out_ref,
@@ -117,6 +120,8 @@
             parts[c][h] = sums.astype(BF16).reshape(n, 16, (b - a) * 256)
             for s, (far, stop) in enumerate(ahead + behind):
                 send(parts[c].at[h, where(h, turned(far))], relayed[c].at[h, s], rl_sem.at[h, c], along(h, turned(stop)))
+    for c in range(len(chunks)):
+        for h in (0, 1):
             for s, d in enumerate(direct):
                 send(parts[c].at[h, where(h, turned(d))], got1[c].at[h, s], r1_sem.at[h, c], along(h, turned(d)))
     wait(tok_sem.at[0], gathered.at[pl.ds(0, m - 1)])
@@ -198,7 +203,7 @@
 def solution(mesh):
     n = int(round(mesh.shape["gx"] ** 0.5))
     m = mesh.shape["gy"]
-    chunks, groups = cut(n, CHUNKS), cut(n, GROUPS)
+    chunks, groups = cut(n, min(n, CHUNKS)), by_hops(n)
     ahead, behind, direct = routes(n)
     relays = len(ahead) + len(behind)
     arrivals = len(direct) + (2 if relays else 0)

time: 59.9 us -> 59.4 us (level)
  no operation moved by 1% of the time
where the time goes in v4:
time: 59.4 us; the launch traced here: 59.2 us
  Pallas kernels  58.6 us (99%)
  local copies, waits for them, and re-layouts  0.6 us (1%)
    pallas_call x1, Pallas kernels, local(): pl.pallas_call(functools.partial(kernel, n, m, chunks, groups), out_shape...  58.6 us

profile of v4, /device:TPU:1, one launch (start us, length us, event | category | flops | bytes accessed | tf_op | source)
XLA Modules:
  0.0 59.2 jit_solution(11738090965806643136)
XLA Ops:
  0.0 58.6 %feed_forward.1 = bf16[8,256]{1,0:T(8,128)(2,1)S(1)} custom-call(bf16[8,256]{1,0:T(8,128)(2,1)} %tokens_hbm.1, bf16[256,2048]{1,0:T(8,128)(2,1)} %gate_hbm.1, bf16[256,2048]{1,0:T(8,128)(2,1)} %up_hbm.1, f32[16,128]{1,0:T(8,128)} %bitcast.3, f32[16,128]{1,0:T(8,128)} %bitcast.4, bf16[2048,256]{1,0:T(8,128)(2,1)} %down_hbm.1, f32[1,256]{1,0:T(1,128)} %bitcast.5), custom_call_target="tpu_custom_call" | custom-call | tf_op jit(solution)/shard_map/feed_forward/pallas_call | solution.py:214
  58.6 0.6 %copy.9 = bf16[8,256]{1,0:T(8,128)(2,1)} copy(bf16[8,256]{1,0:T(8,128)(2,1)S(1)} %feed_forward.1) | data formatting | bytes 8192

commit v5 on v4

--- a/solution.py
+++ b/solution.py
@@ -40,7 +40,7 @@
     passed, rest = rest[: len(chunks)], rest[len(chunks) :]
     sums1, got2 = rest[:2]
     hidden, rest = rest[2 : 2 + len(groups)], rest[2 + len(groups) :]
-    last, got3, load_sem, tok_sem, rl_sem, r1_sem, r2_sem, g1_sem, g2_sem, f_sem = rest
+    last, got3, load_sem, tok_sem, rl_sem, r1_sem, r2_sem, g1_sem, g2_sem, f_sem, here_sem = rest
     gx, gy = lax.axis_index("gx"), lax.axis_index("gy")
     z, y = gx // n, lax.rem(gx, n)
     to_send = far_first(n) + [0]
@@ -81,9 +81,19 @@
     by_distance = sorted(range(1, m), key=lambda d: -min(d // 2, n - d // 2))
     for d in by_distance:
         pl.semaphore_signal(barrier, inc=1, device_id=along_gy(d), device_id_type=MESH)
+    def order(axis, d):
+        i = where(axis, d)
+        return i if axis else jnp.where(i < n // 2, i, n + n // 2 - 1 - i)
+
+    before = order(0, 0) + order(1, 0)
+    after = 2 * (n - 1) - before
     for d in far_first(n):
         for axis in (0, 1):
-            pl.semaphore_signal(barrier, inc=1, device_id=along(axis, d), device_id_type=MESH)
+
+            @pl.when(order(axis, d) > order(axis, 0))
+            def _():
+                pl.semaphore_signal(barrier, inc=1, device_id=along(axis, d), device_id_type=MESH)
+
 
     for h in (0, 1):
         for p, e in enumerate(to_send):
@@ -95,9 +105,16 @@
     own = tokens_own[...].astype(F32)
     packed[...] = jnp.concatenate([own[:, :128], own[:, 128:]], axis=0).astype(BF16)
     gathered[gy] = packed[...]
-    pl.semaphore_wait(barrier, m - 1 + 2 * (n - 1))
+    pl.semaphore_wait(barrier, m - 1 + before)
     for d in by_distance:
         send(packed, gathered.at[gy], tok_sem, along_gy(d))
+    for d in far_first(n):
+        for axis in (0, 1):
+
+            @pl.when(order(axis, d) < order(axis, 0))
+            def _():
+                pl.semaphore_signal(here_sem, inc=1, device_id=along(axis, d), device_id_type=MESH)
+
     for h in (0, 1):
         for q, e in enumerate(to_keep):
             block = pl.ds(pl.multiple_of((h * n + where(1 - h, e)) * 128, 128), 128)
@@ -112,6 +129,10 @@
     wait(tok_sem.at[1], gathered.at[pl.ds(0, m - 1)])
     wide = gathered[...].astype(F32)
     x = jnp.concatenate([wide[:, :8].reshape(8 * m, 128), wide[:, 8:].reshape(8 * m, 128)], axis=1).astype(BF16)
+
+    @pl.when(after > 0)
+    def _():
+        pl.semaphore_wait(here_sem, after)
 
     ahead, behind, direct = routes(n)
     for c, (a, b) in enumerate(chunks):
@@ -242,6 +263,7 @@
                 dma((2, n, 2)),
                 dma((2, len(groups), 2)),
                 dma((2,)),
+                pltpu.SemaphoreType.REGULAR,
             ],
             compiler_params=pltpu.CompilerParams(
                 collective_id=0, has_side_effects=True, vmem_limit_bytes=60 << 20

time: 59.4 us -> 59.7 us (level)
  no operation moved by 1% of the time
where the time goes in v5:
time: 59.7 us; the launch traced here: 59.5 us
  Pallas kernels  58.9 us (99%)
  local copies, waits for them, and re-layouts  0.6 us (1%)
    pallas_call x1, Pallas kernels, local(): pl.pallas_call(functools.partial(kernel, n, m, chunks, groups), out_shape...  58.9 us

profile of v5, /device:TPU:1, one launch (start us, length us, event | category | flops | bytes accessed | tf_op | source)
XLA Modules:
  0.0 59.5 jit_solution(6785347927470702411)
XLA Ops:
  0.0 58.9 %feed_forward.1 = bf16[8,256]{1,0:T(8,128)(2,1)S(1)} custom-call(bf16[8,256]{1,0:T(8,128)(2,1)} %tokens_hbm.1, bf16[256,2048]{1,0:T(8,128)(2,1)} %gate_hbm.1, bf16[256,2048]{1,0:T(8,128)(2,1)} %up_hbm.1, f32[16,128]{1,0:T(8,128)} %bitcast.3, f32[16,128]{1,0:T(8,128)} %bitcast.4, bf16[2048,256]{1,0:T(8,128)(2,1)} %down_hbm.1, f32[1,256]{1,0:T(1,128)} %bitcast.5), custom_call_target="tpu_custom_call" | custom-call | tf_op jit(solution)/shard_map/feed_forward/pallas_call | solution.py:235
  58.9 0.6 %copy.9 = bf16[8,256]{1,0:T(8,128)(2,1)} copy(bf16[8,256]{1,0:T(8,128)(2,1)S(1)} %feed_forward.1) | data formatting | bytes 8192

commit v6 on v4

--- a/solution.py
+++ b/solution.py
@@ -29,7 +29,7 @@
     return [(n * k // parts, n * (k + 1) // parts) for k in range(parts)]
 
 
-CHUNKS = 4
+CHUNKS = 3
 
 
 def kernel(n, m, chunks, groups, tokens_hbm, gate_hbm, up_hbm, gate_scale_hbm, up_scale_hbm, down_hbm, down_scale_hbm, out_ref,
@@ -85,12 +85,6 @@
         for axis in (0, 1):
             pl.semaphore_signal(barrier, inc=1, device_id=along(axis, d), device_id_type=MESH)
 
-    for h in (0, 1):
-        for p, e in enumerate(to_send):
-            block = pl.ds(pl.multiple_of((h * n + where(1 - h, e)) * 128, 128), 128)
-            pltpu.make_async_copy(gate_hbm.at[:, block], weights.at[h, :, pl.ds(p * 256, 128)], load_sem.at[1]).start()
-            pltpu.make_async_copy(up_hbm.at[:, block], weights.at[h, :, pl.ds(p * 256 + 128, 128)], load_sem.at[1]).start()
-
     load_tokens.wait()
     own = tokens_own[...].astype(F32)
     packed[...] = jnp.concatenate([own[:, :128], own[:, 128:]], axis=0).astype(BF16)
@@ -98,6 +92,12 @@
     pl.semaphore_wait(barrier, m - 1 + 2 * (n - 1))
     for d in by_distance:
         send(packed, gathered.at[gy], tok_sem, along_gy(d))
+
+    for h in (0, 1):
+        for p, e in enumerate(to_send):
+            block = pl.ds(pl.multiple_of((h * n + where(1 - h, e)) * 128, 128), 128)
+            pltpu.make_async_copy(gate_hbm.at[:, block], weights.at[h, :, pl.ds(p * 256, 128)], load_sem.at[1]).start()
+            pltpu.make_async_copy(up_hbm.at[:, block], weights.at[h, :, pl.ds(p * 256 + 128, 128)], load_sem.at[1]).start()
     for h in (0, 1):
         for q, e in enumerate(to_keep):
             block = pl.ds(pl.multiple_of((h * n + where(1 - h, e)) * 128, 128), 128)

time: 59.4 us -> 59.3 us (level)
  no operation moved by 1% of the time
where the time goes in v6:
time: 59.3 us; the launch traced here: 59.1 us
  Pallas kernels  58.5 us (99%)
  local copies, waits for them, and re-layouts  0.6 us (1%)
    pallas_call x1, Pallas kernels, local(): pl.pallas_call(functools.partial(kernel, n, m, chunks, groups), out_shape...  58.5 us

profile of v6, /device:TPU:1, one launch (start us, length us, event | category | flops | bytes accessed | tf_op | source)
XLA Modules:
  0.0 59.1 jit_solution(10480516822688220884)
XLA Ops:
  0.0 58.5 %feed_forward.1 = bf16[8,256]{1,0:T(8,128)(2,1)S(1)} custom-call(bf16[8,256]{1,0:T(8,128)(2,1)} %tokens_hbm.1, bf16[256,2048]{1,0:T(8,128)(2,1)} %gate_hbm.1, bf16[256,2048]{1,0:T(8,128)(2,1)} %up_hbm.1, f32[16,128]{1,0:T(8,128)} %bitcast.3, f32[16,128]{1,0:T(8,128)} %bitcast.4, bf16[2048,256]{1,0:T(8,128)(2,1)} %down_hbm.1, f32[1,256]{1,0:T(1,128)} %bitcast.5), custom_call_target="tpu_custom_call" | custom-call | tf_op jit(solution)/shard_map/feed_forward/pallas_call | solution.py:214
  58.5 0.6 %copy.9 = bf16[8,256]{1,0:T(8,128)(2,1)} copy(bf16[8,256]{1,0:T(8,128)(2,1)S(1)} %feed_forward.1) | data formatting | bytes 8192
